TPU v7x, 256 devices: a whole 4x4x8 slice. The times are simulated.
256 devices in a mesh: acq: 8 (over y, z_lo), tile: 32 (over x, z_hi, core).
Axes of the slice: x: 4, y: 4, z: 8 (z_hi: 4, z_lo: 2; z = z_hi * 2 + z_lo), core: 2. Of those that a mesh axis runs over, the one named last changes fastest.
Arguments:
- unprocessed_echo_data: float32 [2, 8, 768, 12288], P(None, 'acq', 'tile'), may hold values from -6 to 6
- slant_kernel_frequencies: float32 [2, 8, 12288], P(None, 'acq'), may hold values from -6 to 6
- along_track_kernel_angle: float32 [8, 768, 12288], P('acq', None, 'tile'), may hold values from -3.140625 to 3.140625
- pairs: int32 [2, 8], replicated, may hold values from 0 to 7, as said below
Outputs:
- interferogram: float32 [2, 2, 8, 128, 1536], P(None, None, 'acq', 'tile')
Inputs may be any that keep to these rules, and one draw needn't show every extreme that they name: `pairs`: in each of the 2 rounds the partners of the 8 acquisitions are a permutation of them; an acquisition may be its own partner.
All inputs are finite; a program needn't handle non-finite values.
Results may differ from a plain program's by a relative error of at most 0.000098.
Values sent between devices are 32-bit elements; how exact they have to be, the bound alone decides.
A program may use at most 128 MiB of HBM per device.

v0:
```python
import jax
import jax.numpy as jnp
import ml_dtypes
import numpy as np
from jax import lax
from jax.experimental import pallas as pl
from jax.experimental.pallas import tpu as pltpu
from jax.sharding import PartitionSpec as P

MESH = pl.DeviceIdType.MESH
NA, NR, AOI, AOI_START = 768, 12288, 256, 256
NP, NQ = 96, 128
NB = 256
ACQ, TILE = 8, 32
GROUPS = 3
CHUNKS = 3
FIRST = AOI_START // 3
KEPT = 88
PART = AOI // ACQ
DESTS = TILE


def split3(matrix):
    high = matrix.astype(ml_dtypes.bfloat16)
    low = (matrix - high.astype(np.float64)).astype(ml_dtypes.bfloat16)
    return np.concatenate([high, high, low], axis=1).astype(np.float32)


def dft_block(size):
    ids = np.arange(size)
    angle = 2.0 * np.pi * (np.outer(ids, ids) % size) / size
    c, s = np.cos(angle), np.sin(angle)
    return np.block([[c, s], [-s, c]])


def tables():
    left_p = split3(dft_block(NP))
    right_q = dft_block(NQ).T.astype(np.float32)
    left_b = dft_block(NB).astype(np.float32)
    angle = 2.0 * np.pi * np.outer(np.arange(NP), np.arange(NQ)) / NR
    twist = np.stack([np.cos(angle), -np.sin(angle)]).astype(np.float32)
    column = np.zeros((NB, 128), np.float64)
    ids = np.arange(NB)
    for a in (1, 2):
        column[:, 2 * a - 2] = np.cos(2.0 * np.pi * a * ids / NA)
        column[:, 2 * a - 1] = -np.sin(2.0 * np.pi * a * ids / NA)
    pool = np.zeros((CHUNKS, 2, 128, 128), np.float32)
    for j in range(CHUNKS):
        for c in range(2):
            for n in range(128):
                pool[j, c, n, 64 * c + 16 * j + n // 8] = 1.0 / 16.0
    return left_p, right_q, left_b, twist, column.astype(np.float32), pool.reshape(CHUNKS, 256, 128)


def halves(value):
    high = value.astype(jnp.bfloat16)
    return high, (value - high.astype(jnp.float32)).astype(jnp.bfloat16)


def left_product(table, value):
    high, low = halves(value)
    rhs = jnp.concatenate([high, low, high], axis=0)
    return jnp.dot(table, rhs, preferred_element_type=jnp.float32)


def right_product(value, table):
    high, low = halves(value)
    lhs = jnp.concatenate([high, low, high], axis=1)
    return jnp.dot(lhs, table, preferred_element_type=jnp.float32)


def kernel(
    pairs, echo, filt, angle, left_p_h, right_q_h, left_b_h, twist_h, column_h, pool_h,
    out,
    x, s, r, cs, ang, foc, gat0, gat1, gat2, cross, osend, orecv,
    fil_raw, fil, left_p_f, right_q_f, left_b_f, left_p, right_q, left_b, left_k, twist, column, pool,
    in_sem, turn_send, turn_recv, turn_own, acq_send, acq_recv, acq_own, out_send, out_recv, out_own,
):
    me_a, me_t = lax.axis_index("acq"), lax.axis_index("tile")
    gat = (gat0, gat1, gat2)

    early = [
        pltpu.make_async_copy(left_p_h, left_p_f, in_sem.at[0]),
        pltpu.make_async_copy(right_q_h, right_q_f, in_sem.at[1]),
        pltpu.make_async_copy(filt, fil_raw, in_sem.at[2]),
        pltpu.make_async_copy(echo, x, in_sem.at[3]),
        pltpu.make_async_copy(twist_h, twist, in_sem.at[4]),
    ]
    late = [
        *[
            pltpu.make_async_copy(angle.at[:, pl.ds(128 * j, 128)], ang.at[j], in_sem.at[10 + j])
            for j in range(CHUNKS)
        ],
        pltpu.make_async_copy(left_b_h, left_b_f, in_sem.at[7]),
        pltpu.make_async_copy(column_h, column, in_sem.at[8]),
        pltpu.make_async_copy(pool_h, pool, in_sem.at[9]),
    ]
    for copy in early + late:
        copy.start()

    barrier = pltpu.get_barrier_semaphore()

    def greet_tile(k, _):
        peer = lax.rem(me_t + k, TILE)
        pl.semaphore_signal(barrier, inc=1, device_id={"tile": peer}, device_id_type=MESH)
        return 0

    def greet_acq(k, _):
        peer = lax.rem(me_a + k, ACQ)
        pl.semaphore_signal(barrier, inc=1, device_id={"acq": peer}, device_id_type=MESH)
        return 0

    def greet_source(k, _):
        source_a = me_t // 4

        @pl.when(jnp.logical_or(source_a != me_a, k != me_t))
        def _():
            pl.semaphore_signal(
                barrier, inc=1, device_id={"acq": source_a, "tile": k}, device_id_type=MESH
            )

        return 0

    lax.fori_loop(1, TILE, greet_tile, 0)
    lax.fori_loop(1, ACQ, greet_acq, 0)
    lax.fori_loop(0, TILE, greet_source, 0)
    early[0].wait()
    left_p[...] = left_p_f[...].astype(jnp.bfloat16)
    early[1].wait()
    high, low = halves(right_q_f[...])
    right_q[...] = jnp.concatenate([high, high, low], axis=0)
    early[2].wait()
    for c in range(2):
        fil[c] = fil_raw[c].T
    early[3].wait()
    early[4].wait()

    def compress(g):
        for part in range(2):
            ids = range(4 * part, 4 * part + 4)
            value = jnp.concatenate(
                [
                    jnp.concatenate([x[c, (3 * i + g) // 8, pl.ds((3 * i + g) % 8, NP, stride=8), :] for i in ids], axis=1)
                    for c in range(2)
                ],
                axis=0,
            )
            value = left_product(left_p[...], value)
            tr, ti = twist[0], twist[1]
            rows = []
            for n in range(4):
                re = value[:NP, n * NQ : (n + 1) * NQ]
                im = value[NP:, n * NQ : (n + 1) * NQ]
                rows.append(jnp.concatenate([re * tr - im * ti, re * ti + im * tr], axis=1))
            value = right_product(jnp.concatenate(rows, axis=0), right_q[...])
            fr, fi = fil[0], fil[1]
            rows = []
            for n in range(4):
                re = value[n * NP : (n + 1) * NP, :NQ]
                im = value[n * NP : (n + 1) * NP, NQ:]
                rows.append(jnp.concatenate([re * fi + im * fr, re * fr - im * fi], axis=1))
            value = right_product(jnp.concatenate(rows, axis=0), right_q[...])
            top, low = [], []
            for n in range(4):
                im = value[n * NP : (n + 1) * NP, :NQ]
                re = value[n * NP : (n + 1) * NP, NQ:]
                top.append(im * tr - re * ti)
                low.append(re * tr + im * ti)
            value = jnp.concatenate(
                [jnp.concatenate(top, axis=1), jnp.concatenate(low, axis=1)], axis=0
            )
            value = left_product(left_p[...], value)
            for n, i in enumerate(ids):
                s[g, 1, pl.ds(i, NP, stride=8), :] = value[:NP, n * NQ : (n + 1) * NQ]
                s[g, 0, pl.ds(i, NP, stride=8), :] = value[NP:, n * NQ : (n + 1) * NQ]

    def turn(j, groups):
        def send(k, _):
            peer = lax.rem(me_t + k, TILE)
            pltpu.make_async_remote_copy(
                src_ref=s.at[groups, :, pl.ds((CHUNKS * peer + j) * 8, 8), :],
                dst_ref=r.at[j, groups, :, pl.ds(me_t * 8, 8), :],
                send_sem=turn_send.at[j],
                recv_sem=turn_recv.at[j],
                device_id={"tile": peer},
                device_id_type=MESH,
            ).start()
            return 0

        lax.fori_loop(1, TILE, send, 0)

    def own_turn(j):
        return pltpu.make_async_copy(
            s.at[:, :, pl.ds((CHUNKS * me_t + j) * 8, 8), :],
            r.at[j, :, :, pl.ds(me_t * 8, 8), :],
            turn_own.at[j],
        )

    for g in range(GROUPS):
        compress(g)
        if g == 0:
            own_is_dest = (me_t // 4 == me_a).astype(jnp.int32)
            pl.semaphore_wait(barrier, (TILE - 1) + (ACQ - 1) + DESTS - own_is_dest)
        turn(0, pl.ds(g, 1))
    for j in range(1, CHUNKS):
        turn(j, pl.ds(0, GROUPS))
    for j in range(CHUNKS):
        own_turn(j).start()
    for copy in late:
        copy.wait()
    high, low = halves(left_b_f[...])
    left_b[...] = jnp.concatenate([high, high, low], axis=1)
    kept = jnp.concatenate(
        [left_b_f[FIRST : FIRST + KEPT, :], left_b_f[NB + FIRST : NB + FIRST + KEPT, :]], axis=0
    )
    high, low = halves(kept)
    left_k[...] = jnp.concatenate([high, high, low], axis=1)

    def phases(j):
        for h in range(12):
            rows = pl.ds(h * 64, 64)
            a = ang[j, rows, :]
            cs[j, 0, rows, :] = jnp.cos(a) * (1.0 / NA / NR)
            cs[j, 1, rows, :] = jnp.sin(a) * (1.0 / NA / NR)

    root = float(np.sqrt(0.75))

    def butterfly(re, im, sign):
        sr, si = re[1] + re[2], im[1] + im[2]
        dr, di = (re[1] - re[2]) * (sign * root), (im[1] - im[2]) * (sign * root)
        mr, mi = re[0] - 0.5 * sr, im[0] - 0.5 * si
        return [re[0] + sr, mr - di, mr + di], [im[0] + si, mi + dr, mi - dr]

    def focus(j):
        value = jnp.concatenate(
            [jnp.concatenate([r[j, a, c] for a in range(3)], axis=1) for c in range(2)], axis=0
        )
        value = left_product(left_b[...], value)
        re = [value[:NB, a * 128 : (a + 1) * 128] for a in range(3)]
        im = [value[NB:, a * 128 : (a + 1) * 128] for a in range(3)]
        for a in (1, 2):
            tr, ti = column[:, 2 * a - 2 : 2 * a - 1], column[:, 2 * a - 1 : 2 * a]
            re[a], im[a] = re[a] * tr - im[a] * ti, re[a] * ti + im[a] * tr
        re, im = butterfly(re, im, -1.0)
        for f1 in range(3):
            c, d = cs[j, 0, f1 * NB : (f1 + 1) * NB, :], cs[j, 1, f1 * NB : (f1 + 1) * NB, :]
            re[f1], im[f1] = re[f1] * c - im[f1] * d, re[f1] * d + im[f1] * c
        re, im = butterfly(re, im, 1.0)
        for a in (1, 2):
            tr, ti = column[:, 2 * a - 2 : 2 * a - 1], column[:, 2 * a - 1 : 2 * a]
            re[a], im[a] = re[a] * tr + im[a] * ti, im[a] * tr - re[a] * ti
        value = jnp.concatenate([jnp.concatenate(im, axis=1), jnp.concatenate(re, axis=1)], axis=0)
        value = left_product(left_k[...], value)
        for a in range(3):
            rows = pl.ds(8 + 3 * FIRST + a - AOI_START, 86, stride=3)
            foc[j, 1, rows, :] = value[:86, a * 128 : (a + 1) * 128]
            foc[j, 0, rows, :] = value[KEPT : KEPT + 86, a * 128 : (a + 1) * 128]

    def own_share(j):
        return pltpu.make_async_copy(
            foc.at[j, :, pl.ds(8 + me_a * PART, PART), :], gat[j].at[me_a], acq_own.at[j]
        )

    def share(j):
        def send(k, _):
            peer = lax.rem(me_a + k, ACQ)
            pltpu.make_async_remote_copy(
                src_ref=foc.at[j, :, pl.ds(8 + peer * PART, PART), :],
                dst_ref=gat[j].at[me_a],
                send_sem=acq_send.at[j],
                recv_sem=acq_recv.at[j],
                device_id={"acq": peer},
                device_id_type=MESH,
            ).start()
            return 0

        lax.fori_loop(1, ACQ, send, 0)
        own_share(j).start()

    def take_share(j):
        whole = gat[j].at[pl.ds(0, ACQ - 1)]
        pltpu.make_async_copy(whole, whole, acq_recv.at[j]).wait()
        own_share(j).wait()

    def interfere(j):
        def one(a, _):
            mine = [[gat[j][a, c, pl.ds(o, 16, stride=2), :] for o in (0, 1)] for c in range(2)]
            for round_id in range(2):
                b = pairs[round_id, a]
                other = [[gat[j][b, c, pl.ds(o, 16, stride=2), :] for o in (0, 1)] for c in range(2)]
                re = sum(mine[c][o] * other[c][o] for c in range(2) for o in range(2))
                im = sum(mine[1][o] * other[0][o] - mine[0][o] * other[1][o] for o in range(2))
                for i in range(4):
                    cross[0, a, i, 4 * round_id : 4 * round_id + 4, :] = re[4 * i : 4 * i + 4]
                    cross[1, a, i, 4 * round_id : 4 * round_id + 4, :] = im[4 * i : 4 * i + 4]
            return 0

        lax.fori_loop(0, ACQ, one, 0)
        re_high, re_low = halves(cross[0].reshape(DESTS * 8, 128))
        im_high, im_low = halves(cross[1].reshape(DESTS * 8, 128))
        lhs = jnp.concatenate([re_high, im_high, re_low, im_low], axis=1)
        sums = pool[j].astype(jnp.bfloat16)
        sums = jnp.concatenate([sums, sums], axis=0)
        looked = jnp.dot(lhs, sums, preferred_element_type=jnp.float32)
        if j == 0:
            osend[...] = looked
        else:
            osend[...] += looked

    phases(0)
    for j in range(CHUNKS):
        if j + 1 < CHUNKS:
            phases(j + 1)
        own_turn(j).wait()
        whole = r.at[j, :, :, pl.ds(0, (TILE - 1) * 8), :]
        pltpu.make_async_copy(whole, whole, turn_recv.at[j]).wait()
        focus(j)
        share(j)
        if j:
            take_share(j - 1)
            interfere(j - 1)
    take_share(CHUNKS - 1)
    interfere(CHUNKS - 1)

    def send_out(d, _):
        dest_a, dest_t = d // 4, 4 * me_a + lax.rem(d, 4)
        own = jnp.logical_and(dest_a == me_a, dest_t == me_t)

        @pl.when(jnp.logical_not(own))
        def _():
            pltpu.make_async_remote_copy(
                src_ref=osend.at[pl.ds(8 * d, 8), :],
                dst_ref=orecv.at[pl.ds(8 * me_t, 8), :],
                send_sem=out_send,
                recv_sem=out_recv,
                device_id={"acq": dest_a, "tile": dest_t},
                device_id_type=MESH,
            ).start()

        return 0

    lax.fori_loop(0, DESTS, send_out, 0)
    has_own = me_t // 4 == me_a

    def out_wait(sem, count):
        whole = orecv.at[pl.ds(0, 8 * count), :]
        pltpu.make_async_copy(whole, whole, sem).wait()

    @pl.when(has_own)
    def _():
        d = 4 * me_a + lax.rem(me_t, 4)
        copy = pltpu.make_async_copy(
            osend.at[pl.ds(8 * d, 8), :], orecv.at[pl.ds(8 * me_t, 8), :], out_own
        )
        copy.start()
        copy.wait()
        out_wait(out_recv, DESTS - 1)
        out_wait(out_send, DESTS - 1)

    @pl.when(jnp.logical_not(has_own))
    def _():
        out_wait(out_recv, DESTS)
        out_wait(out_send, DESTS)

    lane = lax.broadcasted_iota(jnp.int32, (8, 128), 1)
    for c in range(2):
        for v in range(12):
            total = jnp.zeros((8, 128), jnp.float32)
            for t in range((128 * v) // 48, (128 * v + 127) // 48 + 1):
                start = 48 * t - 128 * v
                moved = pltpu.roll(orecv[8 * t : 8 * t + 8, :], (start - 64 * c) % 128, 1)
                inside = jnp.logical_and(lane >= start, lane < start + 48)
                total = jnp.where(inside, moved, total)
            for round_id in range(2):
                out[c, round_id, 0, :, 128 * v : 128 * (v + 1)] = total[4 * round_id : 4 * round_id + 4]

    for j in range(CHUNKS):
        whole = r.at[j, :, :, pl.ds(0, (TILE - 1) * 8), :]
        pltpu.make_async_copy(whole, whole, turn_send.at[j]).wait()
        whole = gat[j].at[pl.ds(0, ACQ - 1)]
        pltpu.make_async_copy(whole, whole, acq_send.at[j]).wait()


def shards(unprocessed_echo_data, slant_kernel_frequencies, along_track_kernel_angle, pairs):
    echo = unprocessed_echo_data.reshape(2, GROUPS, 8, NP, NQ)
    echo = echo.transpose(0, 1, 3, 2, 4).reshape(2, GROUPS, NP * 8, NQ)
    filt = slant_kernel_frequencies.reshape(2, NQ, NP)
    angle = along_track_kernel_angle[0]
    consts = [jnp.asarray(t) for t in tables()]
    any_spec = pl.BlockSpec(memory_space=pl.ANY)
    f32 = jnp.float32
    vmem, dma = pltpu.VMEM, pltpu.SemaphoreType.DMA
    return pl.pallas_call(
        kernel,
        out_shape=jax.ShapeDtypeStruct((2, 2, 1, 4, NR // 8), f32),
        in_specs=[pl.BlockSpec(memory_space=pltpu.SMEM)] + [any_spec] * 9,
        out_specs=pl.BlockSpec(memory_space=pltpu.VMEM),
        scratch_shapes=[
            vmem((2, GROUPS, NP * 8, NQ), f32),
            vmem((GROUPS, 2, NP * 8, NQ), f32),
            vmem((CHUNKS, GROUPS, 2, NB, 128), f32),
            vmem((CHUNKS, 2, NA, 128), f32),
            vmem((CHUNKS, NA, 128), f32),
            vmem((CHUNKS, 2, AOI + 16, 128), f32),
            vmem((ACQ, 2, PART, 128), f32),
            vmem((ACQ, 2, PART, 128), f32),
            vmem((ACQ, 2, PART, 128), f32),
            vmem((2, ACQ, 4, 8, 128), f32),
            vmem((DESTS * 8, 128), f32),
            vmem((DESTS * 8, 128), f32),
            vmem((2, NQ, NP), f32),
            vmem((2, NP, NQ), f32),
            vmem((2 * NP, 6 * NP), f32),
            vmem((2 * NQ, 2 * NQ), f32),
            vmem((2 * NB, 2 * NB), f32),
            vmem((2 * NP, 6 * NP), jnp.bfloat16),
            vmem((6 * NQ, 2 * NQ), jnp.bfloat16),
            vmem((2 * NB, 6 * NB), jnp.bfloat16),
            vmem((2 * KEPT, 6 * NB), jnp.bfloat16),
            vmem((2, NP, NQ), f32),
            vmem((NB, 128), f32),
            vmem((CHUNKS, 2 * 128, 128), f32),
            dma((13,)),
            dma((CHUNKS,)),
            dma((CHUNKS,)),
            dma((CHUNKS,)),
            dma((CHUNKS,)),
            dma((CHUNKS,)),
            dma((CHUNKS,)),
            dma,
            dma,
            dma,
        ],
        name="range_doppler",
        compiler_params=pltpu.CompilerParams(
            collective_id=0, has_side_effects=True, vmem_limit_bytes=56 * 2**20
        ),
    )(pairs, echo, filt, angle, *consts)


def solution(mesh):
    in_specs = (P(None, "acq", "tile", None), P(None, "acq", None), P("acq", None, "tile"), P())
    out_specs = P(None, None, "acq", "tile", None)
    return jax.shard_map(shards, mesh=mesh, in_specs=in_specs, out_specs=out_specs, check_vma=False)
```

profile of v0, /device:TPU:1, one launch (start us, length us, event | category | flops | bytes accessed | tf_op | source)
XLA Modules:
  0.0 88.1 jit_solution(4214382371465301492)
XLA Ops:
  0.0 1.2 %reduce = f32[2,12288]{1,0:T(2,128)S(1)} reduce(f32[2,1,12288]{2,1,0:T(1,128)} %param.11, f32[]{:T(128)} %constant.21), dimensions={1}, to_apply=%param.11.reduce_sub_computation | reduce | bytes 196612 | tf_op args[1]
  1.2 0.8 reshape.11.filt
  2.0 84.6 %range_doppler.1 = f32[2,2,1,4,1536]{4,3,2,1,0:T(4,128)} custom-call(s32[2,8]{1,0:T(2,128)} %pairs.1, f32[2,3,768,128]{3,2,1,0:T(8,128)} %bitcast.6, f32[2,128,96]{2,1,0:T(8,128)} %reshape.11.filt, f32[768,384]{1,0:T(8,128)} %bitcast.7, f32[192,576]{1,0:T(8,128)} %constant.12.clone.left_p_h, f32[256,256]{1,0:T(8,128)} %constant.13.clone.right_q_h, ...), custom_call_target="tpu_custom_call" | custom-call | tf_op jit(solution)/shard_map/range_doppler/pallas_call | solution.py:393
  86.6 1.5 %copy.12 = f32[2,2,1,4,1536]{4,3,2,1,0:T(4,128)} copy(f32[2,2,1,4,1536]{4,3,2,1,0:T(4,128)} %range_doppler.1) | data formatting | bytes 196608
where the time goes:
time: 88.3 us; the launch traced here: 88.1 us
  Pallas kernels  84.6 us (96%)
  local copies, waits for them, and re-layouts  2.33 us (3%)
  other arithmetic  1.18 us (1%)
    pallas_call x1, Pallas kernels, shards(): pl.pallas_call(kernel, out_shape=jax.ShapeDtypeStruct((2, 2, 1, 4, NR //...  84.6 us

commit v1 on v0

--- a/solution.py
+++ b/solution.py
@@ -44,12 +44,7 @@
     for a in (1, 2):
         column[:, 2 * a - 2] = np.cos(2.0 * np.pi * a * ids / NA)
         column[:, 2 * a - 1] = -np.sin(2.0 * np.pi * a * ids / NA)
-    pool = np.zeros((CHUNKS, 2, 128, 128), np.float32)
-    for j in range(CHUNKS):
-        for c in range(2):
-            for n in range(128):
-                pool[j, c, n, 64 * c + 16 * j + n // 8] = 1.0 / 16.0
-    return left_p, right_q, left_b, twist, column.astype(np.float32), pool.reshape(CHUNKS, 256, 128)
+    return left_p, right_q, left_b, twist, column.astype(np.float32)
 
 
 def halves(value):
@@ -70,10 +65,10 @@
 
 
 def kernel(
-    pairs, echo, filt, angle, left_p_h, right_q_h, left_b_h, twist_h, column_h, pool_h,
+    pairs, echo, filt, angle, left_p_h, right_q_h, left_b_h, twist_h, column_h,
     out,
-    x, s, r, cs, ang, foc, gat0, gat1, gat2, cross, osend, orecv,
-    fil_raw, fil, left_p_f, right_q_f, left_b_f, left_p, right_q, left_b, left_k, twist, column, pool,
+    x, s, r, cs, ang, foc, gat0, gat1, gat2, sides, osend, orecv,
+    fil_raw, fil_turn, fil, left_p_f, right_q_f, left_b_f, left_p, right_q, left_b, left_k, twist, column, pool, place,
     in_sem, turn_send, turn_recv, turn_own, acq_send, acq_recv, acq_own, out_send, out_recv, out_own,
 ):
     me_a, me_t = lax.axis_index("acq"), lax.axis_index("tile")
@@ -83,19 +78,18 @@
         pltpu.make_async_copy(left_p_h, left_p_f, in_sem.at[0]),
         pltpu.make_async_copy(right_q_h, right_q_f, in_sem.at[1]),
         pltpu.make_async_copy(filt, fil_raw, in_sem.at[2]),
-        pltpu.make_async_copy(echo, x, in_sem.at[3]),
-        pltpu.make_async_copy(twist_h, twist, in_sem.at[4]),
+        pltpu.make_async_copy(twist_h, twist, in_sem.at[3]),
     ]
+    lines = [pltpu.make_async_copy(echo.at[:, i], x.at[:, i], in_sem.at[4 + i]) for i in range(3)]
     late = [
         *[
-            pltpu.make_async_copy(angle.at[:, pl.ds(128 * j, 128)], ang.at[j], in_sem.at[10 + j])
+            pltpu.make_async_copy(angle.at[:, pl.ds(128 * j, 128)], ang.at[j], in_sem.at[9 + j])
             for j in range(CHUNKS)
         ],
         pltpu.make_async_copy(left_b_h, left_b_f, in_sem.at[7]),
         pltpu.make_async_copy(column_h, column, in_sem.at[8]),
-        pltpu.make_async_copy(pool_h, pool, in_sem.at[9]),
     ]
-    for copy in early + late:
+    for copy in early[:2] + lines[:2] + early[2:] + lines[2:] + late:
         copy.start()
 
     barrier = pltpu.get_barrier_semaphore()
@@ -130,13 +124,26 @@
     high, low = halves(right_q_f[...])
     right_q[...] = jnp.concatenate([high, high, low], axis=0)
     early[2].wait()
+    lane = lax.broadcasted_iota(jnp.int32, (32, 128), 1)
     for c in range(2):
-        fil[c] = fil_raw[c].T
+        v = [fil_raw[c, pl.ds(w, 32, stride=3), :] for w in range(3)]
+        fil_turn[pl.ds(0, 32, stride=4), :] = v[0]
+        fil_turn[pl.ds(1, 32, stride=4), :] = jnp.where(
+            lane < 32, pltpu.roll(v[0], 32, 1), pltpu.roll(v[1], 32, 1)
+        )
+        fil_turn[pl.ds(2, 32, stride=4), :] = jnp.where(
+            lane < 64, pltpu.roll(v[1], 64, 1), pltpu.roll(v[2], 64, 1)
+        )
+        fil_turn[pl.ds(3, 32, stride=4), :] = pltpu.roll(v[2], 96, 1)
+        fil[c] = fil_turn[...].T[:NP]
     early[3].wait()
-    early[4].wait()
+    lines[0].wait()
+    lines[1].wait()
 
     def compress(g):
         for part in range(2):
+            if g == 0 and part == 1:
+                lines[2].wait()
             ids = range(4 * part, 4 * part + 4)
             value = jnp.concatenate(
                 [
@@ -174,20 +181,29 @@
                 s[g, 1, pl.ds(i, NP, stride=8), :] = value[:NP, n * NQ : (n + 1) * NQ]
                 s[g, 0, pl.ds(i, NP, stride=8), :] = value[NP:, n * NQ : (n + 1) * NQ]
 
-    def turn(j, groups):
+    def turn(j, groups, sem):
         def send(k, _):
             peer = lax.rem(me_t + k, TILE)
             pltpu.make_async_remote_copy(
                 src_ref=s.at[groups, :, pl.ds((CHUNKS * peer + j) * 8, 8), :],
                 dst_ref=r.at[j, groups, :, pl.ds(me_t * 8, 8), :],
-                send_sem=turn_send.at[j],
-                recv_sem=turn_recv.at[j],
+                send_sem=turn_send.at[j, sem],
+                recv_sem=turn_recv.at[j, sem],
                 device_id={"tile": peer},
                 device_id_type=MESH,
             ).start()
             return 0
 
         lax.fori_loop(1, TILE, send, 0)
+
+    def turn_wait(j, sems, g=None):
+        if j == 1:
+            whole = r.at[j, :, :, pl.ds(0, (TILE - 1) * 8), :]
+            pltpu.make_async_copy(whole, whole, sems.at[j, 0]).wait()
+        else:
+            for i in range(GROUPS) if g is None else (g,):
+                whole = r.at[j, i, :, pl.ds(0, (TILE - 1) * 8), :]
+                pltpu.make_async_copy(whole, whole, sems.at[j, i]).wait()
 
     def own_turn(j):
         return pltpu.make_async_copy(
@@ -201,9 +217,10 @@
         if g == 0:
             own_is_dest = (me_t // 4 == me_a).astype(jnp.int32)
             pl.semaphore_wait(barrier, (TILE - 1) + (ACQ - 1) + DESTS - own_is_dest)
-        turn(0, pl.ds(g, 1))
-    for j in range(1, CHUNKS):
-        turn(j, pl.ds(0, GROUPS))
+        turn(0, pl.ds(g, 1), g)
+    turn(1, pl.ds(0, GROUPS), 0)
+    for g in range(GROUPS):
+        turn(2, pl.ds(g, 1), g)
     for j in range(CHUNKS):
         own_turn(j).start()
     for copy in late:
@@ -215,6 +232,14 @@
     )
     high, low = halves(kept)
     left_k[...] = jnp.concatenate([high, high, low], axis=1)
+    row = lax.broadcasted_iota(jnp.int32, (1024, 128), 0)
+    col = lax.broadcasted_iota(jnp.int32, (1024, 128), 1)
+    same = jnp.logical_and(col // 16 == row // 128, col % 16 == row % 128 // 8)
+    value = jnp.where(same, 1.0 / 16.0, 0.0).astype(jnp.bfloat16)
+    pool[...] = jnp.concatenate([value, value], axis=0)
+    same = jnp.logical_and(col // 16 == row // 128, col % 16 == row % 16)
+    value = jnp.where(same, 1.0, 0.0).astype(jnp.bfloat16)
+    place[...] = jnp.concatenate([value, value], axis=0)
 
     def phases(j):
         for h in range(12):
@@ -232,12 +257,21 @@
         return [re[0] + sr, mr - di, mr + di], [im[0] + si, mi + dr, mi - dr]
 
     def focus(j):
-        value = jnp.concatenate(
-            [jnp.concatenate([r[j, a, c] for a in range(3)], axis=1) for c in range(2)], axis=0
-        )
-        value = left_product(left_b[...], value)
-        re = [value[:NB, a * 128 : (a + 1) * 128] for a in range(3)]
-        im = [value[NB:, a * 128 : (a + 1) * 128] for a in range(3)]
+        if j < CHUNKS - 1:
+            turn_wait(j, turn_recv)
+            value = jnp.concatenate(
+                [jnp.concatenate([r[j, a, c] for a in range(3)], axis=1) for c in range(2)], axis=0
+            )
+            value = left_product(left_b[...], value)
+            re = [value[:NB, a * 128 : (a + 1) * 128] for a in range(3)]
+            im = [value[NB:, a * 128 : (a + 1) * 128] for a in range(3)]
+        else:
+            re, im = [], []
+            for a in range(3):
+                turn_wait(j, turn_recv, a)
+                value = left_product(left_b[...], jnp.concatenate([r[j, a, 0], r[j, a, 1]], axis=0))
+                re.append(value[:NB])
+                im.append(value[NB:])
         for a in (1, 2):
             tr, ti = column[:, 2 * a - 2 : 2 * a - 1], column[:, 2 * a - 1 : 2 * a]
             re[a], im[a] = re[a] * tr - im[a] * ti, re[a] * ti + im[a] * tr
@@ -283,117 +317,136 @@
         own_share(j).wait()
 
     def interfere(j):
-        def one(a, _):
-            mine = [[gat[j][a, c, pl.ds(o, 16, stride=2), :] for o in (0, 1)] for c in range(2)]
-            for round_id in range(2):
-                b = pairs[round_id, a]
-                other = [[gat[j][b, c, pl.ds(o, 16, stride=2), :] for o in (0, 1)] for c in range(2)]
-                re = sum(mine[c][o] * other[c][o] for c in range(2) for o in range(2))
-                im = sum(mine[1][o] * other[0][o] - mine[0][o] * other[1][o] for o in range(2))
-                for i in range(4):
-                    cross[0, a, i, 4 * round_id : 4 * round_id + 4, :] = re[4 * i : 4 * i + 4]
-                    cross[1, a, i, 4 * round_id : 4 * round_id + 4, :] = im[4 * i : 4 * i + 4]
+        def line_up(a, _):
+            rows = pl.ds(pl.multiple_of(a * PART, PART), PART)
+            for c in range(2):
+                sides[2, c, rows, :] = gat[j][a, c]
+                for round_id in range(2):
+                    sides[round_id, c, rows, :] = gat[j][pairs[round_id, a], c]
             return 0
 
-        lax.fori_loop(0, ACQ, one, 0)
-        re_high, re_low = halves(cross[0].reshape(DESTS * 8, 128))
-        im_high, im_low = halves(cross[1].reshape(DESTS * 8, 128))
-        lhs = jnp.concatenate([re_high, im_high, re_low, im_low], axis=1)
-        sums = pool[j].astype(jnp.bfloat16)
-        sums = jnp.concatenate([sums, sums], axis=0)
-        looked = jnp.dot(lhs, sums, preferred_element_type=jnp.float32)
-        if j == 0:
-            osend[...] = looked
-        else:
-            osend[...] += looked
+        lax.fori_loop(0, ACQ, line_up, 0)
+        re, im = [], []
+        for round_id in range(2):
+            for l in range(4):
+                sum_re, sum_im = 0.0, 0.0
+                for o in range(2):
+                    rows = pl.ds(2 * l + o, DESTS, stride=8)
+                    mr, mi = sides[2, 0, rows, :], sides[2, 1, rows, :]
+                    pr, pi = sides[round_id, 0, rows, :], sides[round_id, 1, rows, :]
+                    sum_re += mr * pr + mi * pi
+                    sum_im += mi * pr - mr * pi
+                re.append(sum_re)
+                im.append(sum_im)
+        value = jnp.concatenate([jnp.concatenate(re, axis=1), jnp.concatenate(im, axis=1)], axis=0)
+        looked = jnp.dot(
+            jnp.concatenate(halves(value), axis=1), pool[...], preferred_element_type=jnp.float32
+        )
+        for c in range(2):
+            osend[j, c] = looked[c * DESTS : (c + 1) * DESTS].reshape(DESTS, 1, 128)
+
+    has_own = me_t // 4 == me_a
+
+    def send_out(j):
+        def send(d, _):
+            dest_a, dest_t = d // 4, 4 * me_a + lax.rem(d, 4)
+            own = jnp.logical_and(dest_a == me_a, dest_t == me_t)
+
+            @pl.when(jnp.logical_not(own))
+            def _():
+                pltpu.make_async_remote_copy(
+                    src_ref=osend.at[j, :, d],
+                    dst_ref=orecv.at[j, :, me_t],
+                    send_sem=out_send.at[j],
+                    recv_sem=out_recv.at[j],
+                    device_id={"acq": dest_a, "tile": dest_t},
+                    device_id_type=MESH,
+                ).start()
+
+            return 0
+
+        lax.fori_loop(0, DESTS, send, 0)
+
+        @pl.when(has_own)
+        def _():
+            own_out(j).start()
+
+    def own_out(j):
+        return pltpu.make_async_copy(
+            osend.at[j, :, 4 * me_a + lax.rem(me_t, 4)], orecv.at[j, :, me_t], out_own.at[j]
+        )
+
+    def out_wait(j, sem):
+        def wait(count):
+            whole = orecv.at[j, :, pl.ds(0, count)]
+            pltpu.make_async_copy(whole, whole, sem).wait()
+
+        @pl.when(has_own)
+        def _():
+            wait(DESTS - 1)
+
+        @pl.when(jnp.logical_not(has_own))
+        def _():
+            wait(DESTS)
 
     phases(0)
     for j in range(CHUNKS):
         if j + 1 < CHUNKS:
             phases(j + 1)
         own_turn(j).wait()
-        whole = r.at[j, :, :, pl.ds(0, (TILE - 1) * 8), :]
-        pltpu.make_async_copy(whole, whole, turn_recv.at[j]).wait()
         focus(j)
         share(j)
         if j:
             take_share(j - 1)
             interfere(j - 1)
+            send_out(j - 1)
     take_share(CHUNKS - 1)
     interfere(CHUNKS - 1)
-
-    def send_out(d, _):
-        dest_a, dest_t = d // 4, 4 * me_a + lax.rem(d, 4)
-        own = jnp.logical_and(dest_a == me_a, dest_t == me_t)
-
-        @pl.when(jnp.logical_not(own))
+    send_out(CHUNKS - 1)
+    for j in range(CHUNKS):
+        turn_wait(j, turn_send)
+        whole = gat[j].at[pl.ds(0, ACQ - 1)]
+        pltpu.make_async_copy(whole, whole, acq_send.at[j]).wait()
+        out_wait(j, out_send.at[j])
+    for j in range(CHUNKS):
+        out_wait(j, out_recv.at[j])
+
+        @pl.when(has_own)
         def _():
-            pltpu.make_async_remote_copy(
-                src_ref=osend.at[pl.ds(8 * d, 8), :],
-                dst_ref=orecv.at[pl.ds(8 * me_t, 8), :],
-                send_sem=out_send,
-                recv_sem=out_recv,
-                device_id={"acq": dest_a, "tile": dest_t},
-                device_id_type=MESH,
-            ).start()
-
-        return 0
-
-    lax.fori_loop(0, DESTS, send_out, 0)
-    has_own = me_t // 4 == me_a
-
-    def out_wait(sem, count):
-        whole = orecv.at[pl.ds(0, 8 * count), :]
-        pltpu.make_async_copy(whole, whole, sem).wait()
-
-    @pl.when(has_own)
-    def _():
-        d = 4 * me_a + lax.rem(me_t, 4)
-        copy = pltpu.make_async_copy(
-            osend.at[pl.ds(8 * d, 8), :], orecv.at[pl.ds(8 * me_t, 8), :], out_own
-        )
-        copy.start()
-        copy.wait()
-        out_wait(out_recv, DESTS - 1)
-        out_wait(out_send, DESTS - 1)
-
-    @pl.when(jnp.logical_not(has_own))
-    def _():
-        out_wait(out_recv, DESTS)
-        out_wait(out_send, DESTS)
-
-    lane = lax.broadcasted_iota(jnp.int32, (8, 128), 1)
+            own_out(j).wait()
+
+    which = lax.broadcasted_iota(jnp.int32, (8, 128), 0)
+    mask = lax.broadcasted_iota(jnp.int32, (8, 128), 1) // 16 == which
+    blocks = []
     for c in range(2):
         for v in range(12):
-            total = jnp.zeros((8, 128), jnp.float32)
-            for t in range((128 * v) // 48, (128 * v + 127) // 48 + 1):
-                start = 48 * t - 128 * v
-                moved = pltpu.roll(orecv[8 * t : 8 * t + 8, :], (start - 64 * c) % 128, 1)
-                inside = jnp.logical_and(lane >= start, lane < start + 48)
-                total = jnp.where(inside, moved, total)
+            pieces = [(u // CHUNKS, u % CHUNKS) for u in range(8 * v, 8 * v + 8)]
+            spread = [jnp.where(mask, orecv[j, c, t], 0.0) for t, j in pieces]
+            blocks.append(jnp.concatenate(spread, axis=1))
+    value = jnp.concatenate(blocks, axis=0)
+    value = jnp.dot(
+        jnp.concatenate(halves(value), axis=1), place[...], preferred_element_type=jnp.float32
+    )
+    for c in range(2):
+        for v in range(12):
             for round_id in range(2):
-                out[c, round_id, 0, :, 128 * v : 128 * (v + 1)] = total[4 * round_id : 4 * round_id + 4]
-
-    for j in range(CHUNKS):
-        whole = r.at[j, :, :, pl.ds(0, (TILE - 1) * 8), :]
-        pltpu.make_async_copy(whole, whole, turn_send.at[j]).wait()
-        whole = gat[j].at[pl.ds(0, ACQ - 1)]
-        pltpu.make_async_copy(whole, whole, acq_send.at[j]).wait()
+                first = (c * 12 + v) * 8 + 4 * round_id
+                out[c, round_id, v] = value[first : first + 4]
 
 
 def shards(unprocessed_echo_data, slant_kernel_frequencies, along_track_kernel_angle, pairs):
     echo = unprocessed_echo_data.reshape(2, GROUPS, 8, NP, NQ)
     echo = echo.transpose(0, 1, 3, 2, 4).reshape(2, GROUPS, NP * 8, NQ)
-    filt = slant_kernel_frequencies.reshape(2, NQ, NP)
+    filt = slant_kernel_frequencies.reshape(2, NP, NQ)
     angle = along_track_kernel_angle[0]
     consts = [jnp.asarray(t) for t in tables()]
     any_spec = pl.BlockSpec(memory_space=pl.ANY)
     f32 = jnp.float32
     vmem, dma = pltpu.VMEM, pltpu.SemaphoreType.DMA
-    return pl.pallas_call(
+    blocks = pl.pallas_call(
         kernel,
-        out_shape=jax.ShapeDtypeStruct((2, 2, 1, 4, NR // 8), f32),
-        in_specs=[pl.BlockSpec(memory_space=pltpu.SMEM)] + [any_spec] * 9,
+        out_shape=jax.ShapeDtypeStruct((2, 2, 12, 4, 128), f32),
+        in_specs=[pl.BlockSpec(memory_space=pltpu.SMEM)] + [any_spec] * 8,
         out_specs=pl.BlockSpec(memory_space=pltpu.VMEM),
         scratch_shapes=[
             vmem((2, GROUPS, NP * 8, NQ), f32),
@@ -405,10 +458,11 @@
             vmem((ACQ, 2, PART, 128), f32),
             vmem((ACQ, 2, PART, 128), f32),
             vmem((ACQ, 2, PART, 128), f32),
-            vmem((2, ACQ, 4, 8, 128), f32),
-            vmem((DESTS * 8, 128), f32),
-            vmem((DESTS * 8, 128), f32),
-            vmem((2, NQ, NP), f32),
+            vmem((3, 2, ACQ * PART, 128), f32),
+            vmem((CHUNKS, 2, DESTS, 1, 128), f32),
+            vmem((CHUNKS, 2, DESTS, 1, 128), f32),
+            vmem((2, NP, NQ), f32),
+            vmem((NQ, 128), f32),
             vmem((2, NP, NQ), f32),
             vmem((2 * NP, 6 * NP), f32),
             vmem((2 * NQ, 2 * NQ), f32),
@@ -419,23 +473,25 @@
             vmem((2 * KEPT, 6 * NB), jnp.bfloat16),
             vmem((2, NP, NQ), f32),
             vmem((NB, 128), f32),
-            vmem((CHUNKS, 2 * 128, 128), f32),
-            dma((13,)),
-            dma((CHUNKS,)),
-            dma((CHUNKS,)),
-            dma((CHUNKS,)),
-            dma((CHUNKS,)),
-            dma((CHUNKS,)),
-            dma((CHUNKS,)),
-            dma,
-            dma,
-            dma,
+            vmem((2 * 8 * 128, 128), jnp.bfloat16),
+            vmem((2 * 8 * 128, 128), jnp.bfloat16),
+            dma((12,)),
+            dma((CHUNKS, GROUPS)),
+            dma((CHUNKS, GROUPS)),
+            dma((CHUNKS,)),
+            dma((CHUNKS,)),
+            dma((CHUNKS,)),
+            dma((CHUNKS,)),
+            dma((CHUNKS,)),
+            dma((CHUNKS,)),
+            dma((CHUNKS,)),
         ],
         name="range_doppler",
         compiler_params=pltpu.CompilerParams(
             collective_id=0, has_side_effects=True, vmem_limit_bytes=56 * 2**20
         ),
     )(pairs, echo, filt, angle, *consts)
+    return blocks.transpose(0, 1, 3, 2, 4).reshape(2, 2, 1, 4, NR // 8)
 
 
 def solution(mesh):

time: 88.3 us -> 88.5 us (level)
  Pallas kernels: 84.6 us -> 86.9 us
  other arithmetic: 1.18 us -> 0 us
    pallas_call x1, Pallas kernels: 84.6 us -> 86.9 us  [shards(): pl.pallas_call(kernel, out_shape=jax.ShapeDtypeStruct((2, 2, 12, 4, 128),...]
    unnamed x1 -> x0, other arithmetic: 1.18 us -> none
where the time goes in v1:
time: 88.5 us; the launch traced here: 88.4 us
  Pallas kernels  86.9 us (98%)
  local copies, waits for them, and re-layouts  1.54 us (2%)
    pallas_call x1, Pallas kernels, shards(): pl.pallas_call(kernel, out_shape=jax.ShapeDtypeStruct((2, 2, 12, 4, 128),...  86.9 us

profile of v1, /device:TPU:1, one launch (start us, length us, event | category | flops | bytes accessed | tf_op | source)
XLA Modules:
  0.0 88.4 jit_solution(10907204389911267103)
XLA Ops:
  0.0 86.9 %range_doppler.1 = f32[2,2,12,4,128]{4,3,2,1,0:T(4,128)} custom-call(s32[2,8]{1,0:T(2,128)} %pairs.1, f32[2,3,768,128]{3,2,1,0:T(8,128)} %bitcast.10, f32[2,96,128]{2,1,0:T(8,128)} %bitcast.13, f32[768,384]{1,0:T(8,128)} %bitcast.11, f32[192,576]{1,0:T(8,128)} %constant.10.clone.left_p_h, f32[256,256]{1,0:T(8,128)} %constant.11.clone.right_q_h, ...), custom_call_target="tpu_custom_call" | custom-call | tf_op jit(solution)/shard_map/range_doppler/pallas_call | solution.py:446
  86.9 1.5 %copy.11 = f32[2,2,1,4,1536]{4,3,2,1,0:T(4,128)} copy(f32[2,2,1,4,1536]{4,3,2,1,0:T(4,128)} %bitcast.12) | data formatting | bytes 196608

commit v2 on v1

--- a/solution.py
+++ b/solution.py
@@ -66,13 +66,19 @@
 
 def kernel(
     pairs, echo, filt, angle, left_p_h, right_q_h, left_b_h, twist_h, column_h,
-    out,
+    out_high, out_low,
     x, s, r, cs, ang, foc, gat0, gat1, gat2, sides, osend, orecv,
-    fil_raw, fil_turn, fil, left_p_f, right_q_f, left_b_f, left_p, right_q, left_b, left_k, twist, column, pool, place,
+    fil_raw, fil_turn, fil, left_p_f, right_q_f, left_b_f, left_p, right_q, left_b, left_k, twist, column, pool, place, first_re, first_im,
     in_sem, turn_send, turn_recv, turn_own, acq_send, acq_recv, acq_own, out_send, out_recv, out_own,
 ):
     me_a, me_t = lax.axis_index("acq"), lax.axis_index("tile")
     gat = (gat0, gat1, gat2)
+    outs = (out_high, out_low)
+
+    def part_of(a):
+        return 2 * lax.rem(me_t // 8 + a // 2, 4) + lax.rem(a, 2)
+
+    me_part = part_of(me_a)
 
     early = [
         pltpu.make_async_copy(left_p_h, left_p_f, in_sem.at[0]),
@@ -104,20 +110,8 @@
         pl.semaphore_signal(barrier, inc=1, device_id={"acq": peer}, device_id_type=MESH)
         return 0
 
-    def greet_source(k, _):
-        source_a = me_t // 4
-
-        @pl.when(jnp.logical_or(source_a != me_a, k != me_t))
-        def _():
-            pl.semaphore_signal(
-                barrier, inc=1, device_id={"acq": source_a, "tile": k}, device_id_type=MESH
-            )
-
-        return 0
-
     lax.fori_loop(1, TILE, greet_tile, 0)
     lax.fori_loop(1, ACQ, greet_acq, 0)
-    lax.fori_loop(0, TILE, greet_source, 0)
     early[0].wait()
     left_p[...] = left_p_f[...].astype(jnp.bfloat16)
     early[1].wait()
@@ -181,14 +175,18 @@
                 s[g, 1, pl.ds(i, NP, stride=8), :] = value[:NP, n * NQ : (n + 1) * NQ]
                 s[g, 0, pl.ds(i, NP, stride=8), :] = value[NP:, n * NQ : (n + 1) * NQ]
 
-    def turn(j, groups, sem):
+    blocks = ((pl.ds(0, 1), pl.ds(0, 24)), (pl.ds(1, 2), pl.ds(0, 16)), (pl.ds(1, 2), pl.ds(16, 8)))
+
+    def turn(block):
+        groups, rows = blocks[block]
+
         def send(k, _):
             peer = lax.rem(me_t + k, TILE)
             pltpu.make_async_remote_copy(
-                src_ref=s.at[groups, :, pl.ds((CHUNKS * peer + j) * 8, 8), :],
-                dst_ref=r.at[j, groups, :, pl.ds(me_t * 8, 8), :],
-                send_sem=turn_send.at[j, sem],
-                recv_sem=turn_recv.at[j, sem],
+                src_ref=s.at[groups, :, pl.ds(24 * peer + rows.start, rows.size), :],
+                dst_ref=r.at[groups, :, me_t, rows, :],
+                send_sem=turn_send.at[block],
+                recv_sem=turn_recv.at[block],
                 device_id={"tile": peer},
                 device_id_type=MESH,
             ).start()
@@ -196,33 +194,22 @@
 
         lax.fori_loop(1, TILE, send, 0)
 
-    def turn_wait(j, sems, g=None):
-        if j == 1:
-            whole = r.at[j, :, :, pl.ds(0, (TILE - 1) * 8), :]
-            pltpu.make_async_copy(whole, whole, sems.at[j, 0]).wait()
-        else:
-            for i in range(GROUPS) if g is None else (g,):
-                whole = r.at[j, i, :, pl.ds(0, (TILE - 1) * 8), :]
-                pltpu.make_async_copy(whole, whole, sems.at[j, i]).wait()
-
-    def own_turn(j):
-        return pltpu.make_async_copy(
-            s.at[:, :, pl.ds((CHUNKS * me_t + j) * 8, 8), :],
-            r.at[j, :, :, pl.ds(me_t * 8, 8), :],
-            turn_own.at[j],
-        )
-
-    for g in range(GROUPS):
-        compress(g)
-        if g == 0:
-            own_is_dest = (me_t // 4 == me_a).astype(jnp.int32)
-            pl.semaphore_wait(barrier, (TILE - 1) + (ACQ - 1) + DESTS - own_is_dest)
-        turn(0, pl.ds(g, 1), g)
-    turn(1, pl.ds(0, GROUPS), 0)
-    for g in range(GROUPS):
-        turn(2, pl.ds(g, 1), g)
-    for j in range(CHUNKS):
-        own_turn(j).start()
+    def turn_wait(block, sems):
+        groups, rows = blocks[block]
+        whole = r.at[groups, :, pl.ds(0, TILE - 1), rows, :]
+        pltpu.make_async_copy(whole, whole, sems.at[block]).wait()
+
+    compress(0)
+    pl.semaphore_wait(barrier, (TILE - 1) + (ACQ - 1))
+    turn(0)
+    compress(1)
+    compress(2)
+    turn(1)
+    turn(2)
+    own_turn = pltpu.make_async_copy(
+        s.at[:, :, pl.ds(24 * me_t, 24), :], r.at[:, :, me_t], turn_own
+    )
+    own_turn.start()
     for copy in late:
         copy.wait()
     high, low = halves(left_b_f[...])
@@ -238,8 +225,7 @@
     value = jnp.where(same, 1.0 / 16.0, 0.0).astype(jnp.bfloat16)
     pool[...] = jnp.concatenate([value, value], axis=0)
     same = jnp.logical_and(col // 16 == row // 128, col % 16 == row % 16)
-    value = jnp.where(same, 1.0, 0.0).astype(jnp.bfloat16)
-    place[...] = jnp.concatenate([value, value], axis=0)
+    place[...] = jnp.where(same, 1.0, 0.0).astype(jnp.bfloat16)
 
     def phases(j):
         for h in range(12):
@@ -256,22 +242,26 @@
         mr, mi = re[0] - 0.5 * sr, im[0] - 0.5 * si
         return [re[0] + sr, mr - di, mr + di], [im[0] + si, mi + dr, mi - dr]
 
+    def transform(j, groups):
+        value = jnp.concatenate(
+            [
+                jnp.concatenate(
+                    [r[a, c, :, 8 * j : 8 * j + 8, :].reshape(NB, 128) for a in groups], axis=1
+                )
+                for c in range(2)
+            ],
+            axis=0,
+        )
+        value = left_product(left_b[...], value)
+        parts = [slice(128 * n, 128 * n + 128) for n in range(len(groups))]
+        return [value[:NB, n] for n in parts], [value[NB:, n] for n in parts]
+
     def focus(j):
         if j < CHUNKS - 1:
-            turn_wait(j, turn_recv)
-            value = jnp.concatenate(
-                [jnp.concatenate([r[j, a, c] for a in range(3)], axis=1) for c in range(2)], axis=0
-            )
-            value = left_product(left_b[...], value)
-            re = [value[:NB, a * 128 : (a + 1) * 128] for a in range(3)]
-            im = [value[NB:, a * 128 : (a + 1) * 128] for a in range(3)]
+            re, im = transform(j, (0, 1, 2))
         else:
-            re, im = [], []
-            for a in range(3):
-                turn_wait(j, turn_recv, a)
-                value = left_product(left_b[...], jnp.concatenate([r[j, a, 0], r[j, a, 1]], axis=0))
-                re.append(value[:NB])
-                im.append(value[NB:])
+            re, im = transform(j, (1, 2))
+            re, im = [first_re[...]] + re, [first_im[...]] + im
         for a in (1, 2):
             tr, ti = column[:, 2 * a - 2 : 2 * a - 1], column[:, 2 * a - 1 : 2 * a]
             re[a], im[a] = re[a] * tr - im[a] * ti, re[a] * ti + im[a] * tr
@@ -292,14 +282,14 @@
 
     def own_share(j):
         return pltpu.make_async_copy(
-            foc.at[j, :, pl.ds(8 + me_a * PART, PART), :], gat[j].at[me_a], acq_own.at[j]
+            foc.at[j, :, pl.ds(8 + me_part * PART, PART), :], gat[j].at[me_a], acq_own.at[j]
         )
 
     def share(j):
         def send(k, _):
             peer = lax.rem(me_a + k, ACQ)
             pltpu.make_async_remote_copy(
-                src_ref=foc.at[j, :, pl.ds(8 + peer * PART, PART), :],
+                src_ref=foc.at[j, :, pl.ds(8 + part_of(peer) * PART, PART), :],
                 dst_ref=gat[j].at[me_a],
                 send_sem=acq_send.at[j],
                 recv_sem=acq_recv.at[j],
@@ -345,18 +335,18 @@
         for c in range(2):
             osend[j, c] = looked[c * DESTS : (c + 1) * DESTS].reshape(DESTS, 1, 128)
 
-    has_own = me_t // 4 == me_a
-
-    def send_out(j):
+    has_own = me_t // 4 == me_part
+
+    def send_out(j, first):
         def send(d, _):
-            dest_a, dest_t = d // 4, 4 * me_a + lax.rem(d, 4)
+            dest_a, dest_t = d // 4, 4 * me_part + lax.rem(d, 4)
             own = jnp.logical_and(dest_a == me_a, dest_t == me_t)
 
             @pl.when(jnp.logical_not(own))
             def _():
                 pltpu.make_async_remote_copy(
-                    src_ref=osend.at[j, :, d],
-                    dst_ref=orecv.at[j, :, me_t],
+                    src_ref=osend.at[pl.ds(first, j + 1 - first), :, d],
+                    dst_ref=orecv.at[pl.ds(first, j + 1 - first), :, me_t],
                     send_sem=out_send.at[j],
                     recv_sem=out_recv.at[j],
                     device_id={"acq": dest_a, "tile": dest_t},
@@ -369,16 +359,17 @@
 
         @pl.when(has_own)
         def _():
-            own_out(j).start()
-
-    def own_out(j):
+            own_out(j, first).start()
+
+    def own_out(j, first):
+        some = pl.ds(first, j + 1 - first)
         return pltpu.make_async_copy(
-            osend.at[j, :, 4 * me_a + lax.rem(me_t, 4)], orecv.at[j, :, me_t], out_own.at[j]
+            osend.at[some, :, 4 * me_a + lax.rem(me_t, 4)], orecv.at[some, :, me_t], out_own.at[j]
         )
 
-    def out_wait(j, sem):
+    def out_wait(j, first, sem):
         def wait(count):
-            whole = orecv.at[j, :, pl.ds(0, count)]
+            whole = orecv.at[pl.ds(first, j + 1 - first), :, pl.ds(0, count)]
             pltpu.make_async_copy(whole, whole, sem).wait()
 
         @pl.when(has_own)
@@ -389,49 +380,52 @@
         def _():
             wait(DESTS)
 
-    phases(0)
     for j in range(CHUNKS):
-        if j + 1 < CHUNKS:
-            phases(j + 1)
-        own_turn(j).wait()
+        phases(j)
+    own_turn.wait()
+    turn_wait(0, turn_recv)
+    (first_re[...],), (first_im[...],) = transform(CHUNKS - 1, (0,))
+    turn_wait(1, turn_recv)
+    for j in range(CHUNKS):
+        if j == CHUNKS - 1:
+            turn_wait(2, turn_recv)
         focus(j)
         share(j)
-        if j:
-            take_share(j - 1)
-            interfere(j - 1)
-            send_out(j - 1)
-    take_share(CHUNKS - 1)
-    interfere(CHUNKS - 1)
-    send_out(CHUNKS - 1)
+    for j in range(CHUNKS):
+        take_share(j)
+        interfere(j)
+        if j == 1:
+            send_out(1, 0)
+        if j == 2:
+            send_out(2, 2)
     for j in range(CHUNKS):
         turn_wait(j, turn_send)
         whole = gat[j].at[pl.ds(0, ACQ - 1)]
         pltpu.make_async_copy(whole, whole, acq_send.at[j]).wait()
-        out_wait(j, out_send.at[j])
-    for j in range(CHUNKS):
-        out_wait(j, out_recv.at[j])
+    for j, first in ((1, 0), (2, 2)):
+        out_wait(j, first, out_send.at[j])
+        out_wait(j, first, out_recv.at[j])
 
         @pl.when(has_own)
         def _():
-            own_out(j).wait()
+            own_out(j, first).wait()
 
     which = lax.broadcasted_iota(jnp.int32, (8, 128), 0)
     mask = lax.broadcasted_iota(jnp.int32, (8, 128), 1) // 16 == which
-    blocks = []
+    spreads = []
     for c in range(2):
         for v in range(12):
             pieces = [(u // CHUNKS, u % CHUNKS) for u in range(8 * v, 8 * v + 8)]
             spread = [jnp.where(mask, orecv[j, c, t], 0.0) for t, j in pieces]
-            blocks.append(jnp.concatenate(spread, axis=1))
-    value = jnp.concatenate(blocks, axis=0)
-    value = jnp.dot(
-        jnp.concatenate(halves(value), axis=1), place[...], preferred_element_type=jnp.float32
-    )
-    for c in range(2):
-        for v in range(12):
-            for round_id in range(2):
-                first = (c * 12 + v) * 8 + 4 * round_id
-                out[c, round_id, v] = value[first : first + 4]
+            spreads.append(jnp.concatenate(spread, axis=1))
+    value = jnp.concatenate(spreads, axis=0)
+    for n, part in enumerate(halves(value)):
+        value = jnp.dot(part, place[...], preferred_element_type=jnp.float32)
+        for c in range(2):
+            for v in range(12):
+                for round_id in range(2):
+                    first = (c * 12 + v) * 8 + 4 * round_id
+                    outs[n][c, round_id, v] = value[first : first + 4]
 
 
 def shards(unprocessed_echo_data, slant_kernel_frequencies, along_track_kernel_angle, pairs):
@@ -443,15 +437,15 @@
     any_spec = pl.BlockSpec(memory_space=pl.ANY)
     f32 = jnp.float32
     vmem, dma = pltpu.VMEM, pltpu.SemaphoreType.DMA
-    blocks = pl.pallas_call(
+    high, low = pl.pallas_call(
         kernel,
-        out_shape=jax.ShapeDtypeStruct((2, 2, 12, 4, 128), f32),
+        out_shape=[jax.ShapeDtypeStruct((2, 2, 12, 4, 128), f32)] * 2,
         in_specs=[pl.BlockSpec(memory_space=pltpu.SMEM)] + [any_spec] * 8,
-        out_specs=pl.BlockSpec(memory_space=pltpu.VMEM),
+        out_specs=[pl.BlockSpec(memory_space=pltpu.VMEM)] * 2,
         scratch_shapes=[
             vmem((2, GROUPS, NP * 8, NQ), f32),
             vmem((GROUPS, 2, NP * 8, NQ), f32),
-            vmem((CHUNKS, GROUPS, 2, NB, 128), f32),
+            vmem((GROUPS, 2, TILE, 8 * CHUNKS, 128), f32),
             vmem((CHUNKS, 2, NA, 128), f32),
             vmem((CHUNKS, NA, 128), f32),
             vmem((CHUNKS, 2, AOI + 16, 128), f32),
@@ -474,11 +468,13 @@
             vmem((2, NP, NQ), f32),
             vmem((NB, 128), f32),
             vmem((2 * 8 * 128, 128), jnp.bfloat16),
-            vmem((2 * 8 * 128, 128), jnp.bfloat16),
+            vmem((8 * 128, 128), jnp.bfloat16),
+            vmem((NB, 128), f32),
+            vmem((NB, 128), f32),
             dma((12,)),
-            dma((CHUNKS, GROUPS)),
-            dma((CHUNKS, GROUPS)),
-            dma((CHUNKS,)),
+            dma((CHUNKS,)),
+            dma((CHUNKS,)),
+            dma,
             dma((CHUNKS,)),
             dma((CHUNKS,)),
             dma((CHUNKS,)),
@@ -491,7 +487,11 @@
             collective_id=0, has_side_effects=True, vmem_limit_bytes=56 * 2**20
         ),
     )(pairs, echo, filt, angle, *consts)
-    return blocks.transpose(0, 1, 3, 2, 4).reshape(2, 2, 1, 4, NR // 8)
+
+    def lay_out(value):
+        return value.transpose(0, 1, 3, 2, 4).reshape(2, 2, 1, 4, NR // 8)
+
+    return lay_out(high) + lay_out(low)
 
 
 def solution(mesh):

time: 88.5 us -> 84.9 us (0.959)
  Pallas kernels: 86.9 us -> 83.2 us
  other arithmetic: 0 us -> 1.61 us
  local copies, waits for them, and re-layouts: 1.54 us -> 0 us
    pallas_call x1, Pallas kernels: 86.9 us -> 83.2 us  [shards(): pl.pallas_call(kernel, out_shape=[jax.ShapeDtypeStruct((2, 2, 12, 4, 128)...]
    add x0 -> x1, other arithmetic: none -> 1.61 us  [shards(): return lay_out(high) + lay_out(low)]
    unnamed x1 -> x0, local copies, waits for them, and re-layouts: 1.54 us -> none
where the time goes in v2:
time: 84.9 us; the launch traced here: 84.8 us
  Pallas kernels  83.2 us (98%)
  other arithmetic  1.61 us (2%)
    pallas_call x1, Pallas kernels, shards(): pl.pallas_call(kernel, out_shape=[jax.ShapeDtypeStruct((2, 2, 12, 4, 128)...  83.2 us

profile of v2, /device:TPU:1, one launch (start us, length us, event | category | flops | bytes accessed | tf_op | source)
XLA Modules:
  0.0 84.8 jit_solution(229021810865103276)
XLA Ops:
  0.0 83.2 %range_doppler.1 = (f32[2,2,12,4,128]{4,3,2,1,0:T(4,128)}, f32[2,2,12,4,128]{4,3,2,1,0:T(4,128)}) custom-call(s32[2,8]{1,0:T(2,128)} %pairs.1, f32[2,3,768,128]{3,2,1,0:T(8,128)} %bitcast.11, f32[2,96,128]{2,1,0:T(8,128)} %bitcast.13, f32[768,384]{1,0:T(8,128)} %bitcast.12, f32[192,576]{1,0:T(8,128)} %constant.10.clone.left_p_h, ...), custom_call_target="tpu_custom_call" | custom-call | tf_op jit(solution)/shard_map/range_doppler/pallas_call | solution.py:440
  83.2 1.6 %add_bitcast_fusion = f32[2,2,1,4,1536]{4,3,2,1,0:T(4,128)} fusion(f32[2,2,12,4,128]{4,3,2,1,0:T(4,128)} %get-tuple-element.7, f32[2,2,12,4,128]{4,3,2,1,0:T(4,128)} %get-tuple-element.8), kind=kLoop, calls=%fused_computation | loop fusion | flops 24576 | bytes 294912 | tf_op jit(solution)/shard_map/add | solution.py:494

commit v3 on v2

--- a/solution.py
+++ b/solution.py
@@ -4,6 +4,7 @@
 import numpy as np
 from jax import lax
 from jax.experimental import pallas as pl
+from jax.experimental.layout import Layout, with_layout_constraint
 from jax.experimental.pallas import tpu as pltpu
 from jax.sharding import PartitionSpec as P
 
@@ -68,7 +69,7 @@
     pairs, echo, filt, angle, left_p_h, right_q_h, left_b_h, twist_h, column_h,
     out_high, out_low,
     x, s, r, cs, ang, foc, gat0, gat1, gat2, sides, osend, orecv,
-    fil_raw, fil_turn, fil, left_p_f, right_q_f, left_b_f, left_p, right_q, left_b, left_k, twist, column, pool, place, first_re, first_im,
+    fil_raw, fil_turn, fil, left_p_f, right_q_f, left_b_f, left_p, right_q, left_b, left_k, twist, column, wide, pool, place, first_re, first_im,
     in_sem, turn_send, turn_recv, turn_own, acq_send, acq_recv, acq_own, out_send, out_recv, out_own,
 ):
     me_a, me_t = lax.axis_index("acq"), lax.axis_index("tile")
@@ -79,6 +80,10 @@
         return 2 * lax.rem(me_t // 8 + a // 2, 4) + lax.rem(a, 2)
 
     me_part = part_of(me_a)
+
+    def far_first(k):
+        return 4 + (k + 1) // 2 * (2 * lax.rem(k, 2) - 1)
+
 
     early = [
         pltpu.make_async_copy(left_p_h, left_p_f, in_sem.at[0]),
@@ -212,6 +217,8 @@
     own_turn.start()
     for copy in late:
         copy.wait()
+    for n in range(4):
+        wide[n] = jnp.broadcast_to(column[:, n : n + 1], (NB, 128))
     high, low = halves(left_b_f[...])
     left_b[...] = jnp.concatenate([high, high, low], axis=1)
     kept = jnp.concatenate(
@@ -263,7 +270,7 @@
             re, im = transform(j, (1, 2))
             re, im = [first_re[...]] + re, [first_im[...]] + im
         for a in (1, 2):
-            tr, ti = column[:, 2 * a - 2 : 2 * a - 1], column[:, 2 * a - 1 : 2 * a]
+            tr, ti = wide[2 * a - 2], wide[2 * a - 1]
             re[a], im[a] = re[a] * tr - im[a] * ti, re[a] * ti + im[a] * tr
         re, im = butterfly(re, im, -1.0)
         for f1 in range(3):
@@ -271,7 +278,7 @@
             re[f1], im[f1] = re[f1] * c - im[f1] * d, re[f1] * d + im[f1] * c
         re, im = butterfly(re, im, 1.0)
         for a in (1, 2):
-            tr, ti = column[:, 2 * a - 2 : 2 * a - 1], column[:, 2 * a - 1 : 2 * a]
+            tr, ti = wide[2 * a - 2], wide[2 * a - 1]
             re[a], im[a] = re[a] * tr + im[a] * ti, im[a] * tr - re[a] * ti
         value = jnp.concatenate([jnp.concatenate(im, axis=1), jnp.concatenate(re, axis=1)], axis=0)
         value = left_product(left_k[...], value)
@@ -287,7 +294,7 @@
 
     def share(j):
         def send(k, _):
-            peer = lax.rem(me_a + k, ACQ)
+            peer = lax.rem(me_a + far_first(k), ACQ)
             pltpu.make_async_remote_copy(
                 src_ref=foc.at[j, :, pl.ds(8 + part_of(peer) * PART, PART), :],
                 dst_ref=gat[j].at[me_a],
@@ -298,7 +305,7 @@
             ).start()
             return 0
 
-        lax.fori_loop(1, ACQ, send, 0)
+        lax.fori_loop(0, ACQ - 1, send, 0)
         own_share(j).start()
 
     def take_share(j):
@@ -339,13 +346,14 @@
 
     def send_out(j, first):
         def send(d, _):
-            dest_a, dest_t = d // 4, 4 * me_part + lax.rem(d, 4)
+            dest_a = lax.rem(me_a + far_first(d // 4), ACQ)
+            dest_t = 4 * me_part + lax.rem(d, 4)
             own = jnp.logical_and(dest_a == me_a, dest_t == me_t)
 
             @pl.when(jnp.logical_not(own))
             def _():
                 pltpu.make_async_remote_copy(
-                    src_ref=osend.at[pl.ds(first, j + 1 - first), :, d],
+                    src_ref=osend.at[pl.ds(first, j + 1 - first), :, 4 * dest_a + lax.rem(d, 4)],
                     dst_ref=orecv.at[pl.ds(first, j + 1 - first), :, me_t],
                     send_sem=out_send.at[j],
                     recv_sem=out_recv.at[j],
@@ -419,13 +427,14 @@
             spread = [jnp.where(mask, orecv[j, c, t], 0.0) for t, j in pieces]
             spreads.append(jnp.concatenate(spread, axis=1))
     value = jnp.concatenate(spreads, axis=0)
-    for n, part in enumerate(halves(value)):
+    for out, part in zip(outs, halves(value)):
         value = jnp.dot(part, place[...], preferred_element_type=jnp.float32)
         for c in range(2):
             for v in range(12):
                 for round_id in range(2):
                     first = (c * 12 + v) * 8 + 4 * round_id
-                    outs[n][c, round_id, v] = value[first : first + 4]
+                    rows = (c * 2 + round_id) * 48 + 4 * v
+                    out[rows : rows + 4, :] = value[first : first + 4]
 
 
 def shards(unprocessed_echo_data, slant_kernel_frequencies, along_track_kernel_angle, pairs):
@@ -439,7 +448,7 @@
     vmem, dma = pltpu.VMEM, pltpu.SemaphoreType.DMA
     high, low = pl.pallas_call(
         kernel,
-        out_shape=[jax.ShapeDtypeStruct((2, 2, 12, 4, 128), f32)] * 2,
+        out_shape=[vmem((2 * 2 * 12 * 4, 128), f32)] * 2,
         in_specs=[pl.BlockSpec(memory_space=pltpu.SMEM)] + [any_spec] * 8,
         out_specs=[pl.BlockSpec(memory_space=pltpu.VMEM)] * 2,
         scratch_shapes=[
@@ -467,6 +476,7 @@
             vmem((2 * KEPT, 6 * NB), jnp.bfloat16),
             vmem((2, NP, NQ), f32),
             vmem((NB, 128), f32),
+            vmem((4, NB, 128), f32),
             vmem((2 * 8 * 128, 128), jnp.bfloat16),
             vmem((8 * 128, 128), jnp.bfloat16),
             vmem((NB, 128), f32),
@@ -488,10 +498,9 @@
         ),
     )(pairs, echo, filt, angle, *consts)
 
-    def lay_out(value):
-        return value.transpose(0, 1, 3, 2, 4).reshape(2, 2, 1, 4, NR // 8)
-
-    return lay_out(high) + lay_out(low)
+    rows = (high + low).reshape(2, 2, 12, 4, 128).transpose(0, 1, 3, 2, 4)
+    rows = with_layout_constraint(rows, Layout((0, 1, 3, 2, 4)))
+    return rows.reshape(2, 2, 1, 4, NR // 8)
 
 
 def solution(mesh):

time: 84.9 us -> 83.3 us (0.981)
  other arithmetic: 1.61 us -> 0.65 us
    add x1, other arithmetic: 1.61 us -> 0.65 us  [shards(): rows = (high + low).reshape(2, 2, 12, 4, 128).transpose(0, 1, 3, 2, 4)]
where the time goes in v3:
time: 83.3 us; the launch traced here: 83.2 us
  Pallas kernels  82.6 us (99%)
    pallas_call x1, Pallas kernels, shards(): pl.pallas_call(kernel, out_shape=[vmem((2 * 2 * 12 * 4, 128), f32)] * 2,...  82.6 us

profile of v3, /device:TPU:1, one launch (start us, length us, event | category | flops | bytes accessed | tf_op | source)
XLA Modules:
  0.0 83.2 jit_solution(1909352173815844167)
XLA Ops:
  0.0 82.6 %range_doppler.1 = (f32[192,128]{1,0:T(8,128)S(1)}, f32[192,128]{1,0:T(8,128)S(1)}) custom-call(s32[2,8]{1,0:T(2,128)} %pairs.1, f32[2,3,768,128]{3,2,1,0:T(8,128)} %bitcast.12, f32[2,96,128]{2,1,0:T(8,128)} %bitcast.14, f32[768,384]{1,0:T(8,128)} %bitcast.13, f32[192,576]{1,0:T(8,128)} %constant.10.clone.left_p_h, f32[256,256]{1,0:T(8,128)} %constant.11.clone.right_q_h, ...), custom_call_target="tpu_custom_call" | custom-call | tf_op jit(solution)/shard_map/range_doppler/pallas_call | solution.py:449
  82.6 0.7 add.3

commit v4 on v3

--- a/solution.py
+++ b/solution.py
@@ -67,14 +67,13 @@
 
 def kernel(
     pairs, echo, filt, angle, left_p_h, right_q_h, left_b_h, twist_h, column_h,
-    out_high, out_low,
+    out_early, out_late,
     x, s, r, cs, ang, foc, gat0, gat1, gat2, sides, osend, orecv,
     fil_raw, fil_turn, fil, left_p_f, right_q_f, left_b_f, left_p, right_q, left_b, left_k, twist, column, wide, pool, place, first_re, first_im,
     in_sem, turn_send, turn_recv, turn_own, acq_send, acq_recv, acq_own, out_send, out_recv, out_own,
 ):
     me_a, me_t = lax.axis_index("acq"), lax.axis_index("tile")
     gat = (gat0, gat1, gat2)
-    outs = (out_high, out_low)
 
     def part_of(a):
         return 2 * lax.rem(me_t // 8 + a // 2, 4) + lax.rem(a, 2)
@@ -225,7 +224,7 @@
         [left_b_f[FIRST : FIRST + KEPT, :], left_b_f[NB + FIRST : NB + FIRST + KEPT, :]], axis=0
     )
     high, low = halves(kept)
-    left_k[...] = jnp.concatenate([high, high, low], axis=1)
+    left_k[...] = jnp.concatenate([high, low], axis=0)
     row = lax.broadcasted_iota(jnp.int32, (1024, 128), 0)
     col = lax.broadcasted_iota(jnp.int32, (1024, 128), 1)
     same = jnp.logical_and(col // 16 == row // 128, col % 16 == row % 128 // 8)
@@ -281,7 +280,10 @@
             tr, ti = wide[2 * a - 2], wide[2 * a - 1]
             re[a], im[a] = re[a] * tr + im[a] * ti, im[a] * tr - re[a] * ti
         value = jnp.concatenate([jnp.concatenate(im, axis=1), jnp.concatenate(re, axis=1)], axis=0)
-        value = left_product(left_k[...], value)
+        high, low = halves(value)
+        value = jnp.dot(left_k[...], high, preferred_element_type=jnp.float32)
+        rest = jnp.dot(left_k[: 2 * KEPT], low, preferred_element_type=jnp.float32)
+        value = value[: 2 * KEPT] + (value[2 * KEPT :] + rest)
         for a in range(3):
             rows = pl.ds(8 + 3 * FIRST + a - AOI_START, 86, stride=3)
             foc[j, 1, rows, :] = value[:86, a * 128 : (a + 1) * 128]
@@ -410,31 +412,39 @@
         turn_wait(j, turn_send)
         whole = gat[j].at[pl.ds(0, ACQ - 1)]
         pltpu.make_async_copy(whole, whole, acq_send.at[j]).wait()
-    for j, first in ((1, 0), (2, 2)):
-        out_wait(j, first, out_send.at[j])
+    which = lax.broadcasted_iota(jnp.int32, (8, 128), 0)
+    mask = lax.broadcasted_iota(jnp.int32, (8, 128), 1) // 16 == which
+
+    def arrange(out, chunks):
+        for first_v in range(3):
+            blocks = [(c, v) for c in range(2) for v in range(first_v, 12, 3)]
+            ns = [n for n in range(8) if (8 * first_v + n) % CHUNKS in chunks]
+            rows = []
+            for c, v in blocks:
+                us = [8 * v + n for n in ns]
+                spread = [jnp.where(mask, orecv[u % CHUNKS, c, u // CHUNKS], 0.0) for u in us]
+                rows.append(jnp.concatenate(spread, axis=1))
+            table = jnp.concatenate([place[128 * n : 128 * n + 128] for n in ns], axis=0)
+            high, low = halves(jnp.concatenate(rows, axis=0))
+            value = jnp.dot(high, table, preferred_element_type=jnp.float32)
+            value += jnp.dot(low, table, preferred_element_type=jnp.float32)
+            for n, (c, v) in enumerate(blocks):
+                for round_id in range(2):
+                    row = (c * 2 + round_id) * 48 + 4 * v
+                    first = 8 * n + 4 * round_id
+                    out[row : row + 4, :] = value[first : first + 4]
+
+    for j, first, out, chunks in ((1, 0, out_early, (0, 1)), (2, 2, out_late, (2,))):
         out_wait(j, first, out_recv.at[j])
 
         @pl.when(has_own)
         def _():
             own_out(j, first).wait()
 
-    which = lax.broadcasted_iota(jnp.int32, (8, 128), 0)
-    mask = lax.broadcasted_iota(jnp.int32, (8, 128), 1) // 16 == which
-    spreads = []
-    for c in range(2):
-        for v in range(12):
-            pieces = [(u // CHUNKS, u % CHUNKS) for u in range(8 * v, 8 * v + 8)]
-            spread = [jnp.where(mask, orecv[j, c, t], 0.0) for t, j in pieces]
-            spreads.append(jnp.concatenate(spread, axis=1))
-    value = jnp.concatenate(spreads, axis=0)
-    for out, part in zip(outs, halves(value)):
-        value = jnp.dot(part, place[...], preferred_element_type=jnp.float32)
-        for c in range(2):
-            for v in range(12):
-                for round_id in range(2):
-                    first = (c * 12 + v) * 8 + 4 * round_id
-                    rows = (c * 2 + round_id) * 48 + 4 * v
-                    out[rows : rows + 4, :] = value[first : first + 4]
+        arrange(out, chunks)
+
+    for j, first in ((1, 0), (2, 2)):
+        out_wait(j, first, out_send.at[j])
 
 
 def shards(unprocessed_echo_data, slant_kernel_frequencies, along_track_kernel_angle, pairs):
@@ -446,7 +456,7 @@
     any_spec = pl.BlockSpec(memory_space=pl.ANY)
     f32 = jnp.float32
     vmem, dma = pltpu.VMEM, pltpu.SemaphoreType.DMA
-    high, low = pl.pallas_call(
+    early, late = pl.pallas_call(
         kernel,
         out_shape=[vmem((2 * 2 * 12 * 4, 128), f32)] * 2,
         in_specs=[pl.BlockSpec(memory_space=pltpu.SMEM)] + [any_spec] * 8,
@@ -473,7 +483,7 @@
             vmem((2 * NP, 6 * NP), jnp.bfloat16),
             vmem((6 * NQ, 2 * NQ), jnp.bfloat16),
             vmem((2 * NB, 6 * NB), jnp.bfloat16),
-            vmem((2 * KEPT, 6 * NB), jnp.bfloat16),
+            vmem((4 * KEPT, 2 * NB), jnp.bfloat16),
             vmem((2, NP, NQ), f32),
             vmem((NB, 128), f32),
             vmem((4, NB, 128), f32),
@@ -498,7 +508,7 @@
         ),
     )(pairs, echo, filt, angle, *consts)
 
-    rows = (high + low).reshape(2, 2, 12, 4, 128).transpose(0, 1, 3, 2, 4)
+    rows = (early + late).reshape(2, 2, 12, 4, 128).transpose(0, 1, 3, 2, 4)
     rows = with_layout_constraint(rows, Layout((0, 1, 3, 2, 4)))
     return rows.reshape(2, 2, 1, 4, NR // 8)
 

time: 83.3 us -> 83.2 us (level)
  no operation moved by 1% of the time
where the time goes in v4:
time: 83.2 us; the launch traced here: 83.1 us
  Pallas kernels  82.4 us (99%)
    pallas_call x1, Pallas kernels, shards(): pl.pallas_call(kernel, out_shape=[vmem((2 * 2 * 12 * 4, 128), f32)] * 2,...  82.4 us

profile of v4, /device:TPU:1, one launch (start us, length us, event | category | flops | bytes accessed | tf_op | source)
XLA Modules:
  0.0 83.1 jit_solution(8021134150464564252)
XLA Ops:
  0.0 82.4 %range_doppler.1 = (f32[192,128]{1,0:T(8,128)S(1)}, f32[192,128]{1,0:T(8,128)S(1)}) custom-call(s32[2,8]{1,0:T(2,128)} %pairs.1, f32[2,3,768,128]{3,2,1,0:T(8,128)} %bitcast.12, f32[2,96,128]{2,1,0:T(8,128)} %bitcast.14, f32[768,384]{1,0:T(8,128)} %bitcast.13, f32[192,576]{1,0:T(8,128)} %constant.10.clone.left_p_h, f32[256,256]{1,0:T(8,128)} %constant.11.clone.right_q_h, ...), custom_call_target="tpu_custom_call" | custom-call | tf_op jit(solution)/shard_map/range_doppler/pallas_call | solution.py:459
  82.5 0.7 add.3

commit v5 on v4

--- a/solution.py
+++ b/solution.py
@@ -19,6 +19,7 @@
 KEPT = 88
 PART = AOI // ACQ
 DESTS = TILE
+STEPS = ((0, PART, 0), (1, PART, 0), (2, PART // 2, 0), (2, PART // 2, PART // 2))
 
 
 def split3(matrix):
@@ -68,12 +69,12 @@
 def kernel(
     pairs, echo, filt, angle, left_p_h, right_q_h, left_b_h, twist_h, column_h,
     out_early, out_late,
-    x, s, r, cs, ang, foc, gat0, gat1, gat2, sides, osend, orecv,
+    x, s, r, cs, ang, foc, gat0, gat1, gat2, gat3, sides, osend, osend_last, orecv,
     fil_raw, fil_turn, fil, left_p_f, right_q_f, left_b_f, left_p, right_q, left_b, left_k, twist, column, wide, pool, place, first_re, first_im,
     in_sem, turn_send, turn_recv, turn_own, acq_send, acq_recv, acq_own, out_send, out_recv, out_own,
 ):
     me_a, me_t = lax.axis_index("acq"), lax.axis_index("tile")
-    gat = (gat0, gat1, gat2)
+    gat = (gat0, gat1, gat2, gat3)
 
     def part_of(a):
         return 2 * lax.rem(me_t // 8 + a // 2, 4) + lax.rem(a, 2)
@@ -289,39 +290,43 @@
             foc[j, 1, rows, :] = value[:86, a * 128 : (a + 1) * 128]
             foc[j, 0, rows, :] = value[KEPT : KEPT + 86, a * 128 : (a + 1) * 128]
 
-    def own_share(j):
-        return pltpu.make_async_copy(
-            foc.at[j, :, pl.ds(8 + me_part * PART, PART), :], gat[j].at[me_a], acq_own.at[j]
-        )
-
-    def share(j):
+    def own_share(n):
+        j, lines, first = STEPS[n]
+        rows = pl.ds(8 + me_part * PART + first, lines)
+        return pltpu.make_async_copy(foc.at[j, :, rows, :], gat[n].at[me_a], acq_own.at[n])
+
+    def share(n):
+        j, lines, first = STEPS[n]
+
         def send(k, _):
             peer = lax.rem(me_a + far_first(k), ACQ)
             pltpu.make_async_remote_copy(
-                src_ref=foc.at[j, :, pl.ds(8 + part_of(peer) * PART, PART), :],
-                dst_ref=gat[j].at[me_a],
-                send_sem=acq_send.at[j],
-                recv_sem=acq_recv.at[j],
+                src_ref=foc.at[j, :, pl.ds(8 + part_of(peer) * PART + first, lines), :],
+                dst_ref=gat[n].at[me_a],
+                send_sem=acq_send.at[n],
+                recv_sem=acq_recv.at[n],
                 device_id={"acq": peer},
                 device_id_type=MESH,
             ).start()
             return 0
 
         lax.fori_loop(0, ACQ - 1, send, 0)
-        own_share(j).start()
-
-    def take_share(j):
-        whole = gat[j].at[pl.ds(0, ACQ - 1)]
-        pltpu.make_async_copy(whole, whole, acq_recv.at[j]).wait()
-        own_share(j).wait()
-
-    def interfere(j):
+        own_share(n).start()
+
+    def take_share(n):
+        whole = gat[n].at[pl.ds(0, ACQ - 1)]
+        pltpu.make_async_copy(whole, whole, acq_recv.at[n]).wait()
+        own_share(n).wait()
+
+    def interfere(n):
+        lines = STEPS[n][1]
+
         def line_up(a, _):
-            rows = pl.ds(pl.multiple_of(a * PART, PART), PART)
+            rows = pl.ds(pl.multiple_of(a * lines, lines), lines)
             for c in range(2):
-                sides[2, c, rows, :] = gat[j][a, c]
+                sides[2, c, rows, :] = gat[n][a, c]
                 for round_id in range(2):
-                    sides[round_id, c, rows, :] = gat[j][pairs[round_id, a], c]
+                    sides[round_id, c, rows, :] = gat[n][pairs[round_id, a], c]
             return 0
 
         lax.fori_loop(0, ACQ, line_up, 0)
@@ -330,7 +335,7 @@
             for l in range(4):
                 sum_re, sum_im = 0.0, 0.0
                 for o in range(2):
-                    rows = pl.ds(2 * l + o, DESTS, stride=8)
+                    rows = pl.ds(2 * l + o, lines, stride=8)
                     mr, mi = sides[2, 0, rows, :], sides[2, 1, rows, :]
                     pr, pi = sides[round_id, 0, rows, :], sides[round_id, 1, rows, :]
                     sum_re += mr * pr + mi * pi
@@ -342,21 +347,26 @@
             jnp.concatenate(halves(value), axis=1), pool[...], preferred_element_type=jnp.float32
         )
         for c in range(2):
-            osend[j, c] = looked[c * DESTS : (c + 1) * DESTS].reshape(DESTS, 1, 128)
+            rows = looked[c * lines : (c + 1) * lines].reshape(lines, 1, 128)
+            if n < 2:
+                osend[n, c] = rows
+            else:
+                osend_last[n - 2, c] = rows
 
     has_own = me_t // 4 == me_part
 
-    def send_out(j, first):
+    def send_looks(j, count, source, target):
         def send(d, _):
-            dest_a = lax.rem(me_a + far_first(d // 4), ACQ)
-            dest_t = 4 * me_part + lax.rem(d, 4)
+            dest_a = lax.rem(me_a + far_first(d // count), ACQ)
+            i = target + lax.rem(d, count)
+            dest_t = 4 * me_part + i
             own = jnp.logical_and(dest_a == me_a, dest_t == me_t)
 
             @pl.when(jnp.logical_not(own))
             def _():
                 pltpu.make_async_remote_copy(
-                    src_ref=osend.at[pl.ds(first, j + 1 - first), :, 4 * dest_a + lax.rem(d, 4)],
-                    dst_ref=orecv.at[pl.ds(first, j + 1 - first), :, me_t],
+                    src_ref=source(count * dest_a + i - target),
+                    dst_ref=looks(j),
                     send_sem=out_send.at[j],
                     recv_sem=out_recv.at[j],
                     device_id={"acq": dest_a, "tile": dest_t},
@@ -365,17 +375,27 @@
 
             return 0
 
-        lax.fori_loop(0, DESTS, send, 0)
-
-        @pl.when(has_own)
-        def _():
-            own_out(j, first).start()
-
-    def own_out(j, first):
-        some = pl.ds(first, j + 1 - first)
-        return pltpu.make_async_copy(
-            osend.at[some, :, 4 * me_a + lax.rem(me_t, 4)], orecv.at[some, :, me_t], out_own.at[j]
-        )
+        lax.fori_loop(0, ACQ * count, send, 0)
+
+    def looks(j):
+        return orecv.at[pl.ds(0, 2) if j == 1 else pl.ds(2, 1), :, me_t]
+
+    def send_early():
+        send_looks(1, 4, lambda d: osend.at[:, :, d], 0)
+        pl.when(has_own)(own_out(1).start)
+
+    def send_last(half):
+        send_looks(2, 2, lambda d: osend_last.at[pl.ds(half, 1), :, d], 2 * half)
+        if half == 1:
+            pl.when(has_own)(own_out(2).start)
+
+    def own_out(j):
+        i = lax.rem(me_t, 4)
+        if j == 1:
+            source = osend.at[:, :, 4 * me_a + i]
+        else:
+            source = osend_last.at[pl.ds(i // 2, 1), :, 2 * me_a + lax.rem(i, 2)]
+        return pltpu.make_async_copy(source, looks(j), out_own.at[j])
 
     def out_wait(j, first, sem):
         def wait(count):
@@ -400,18 +420,21 @@
         if j == CHUNKS - 1:
             turn_wait(2, turn_recv)
         focus(j)
-        share(j)
-    for j in range(CHUNKS):
-        take_share(j)
-        interfere(j)
-        if j == 1:
-            send_out(1, 0)
-        if j == 2:
-            send_out(2, 2)
+        for n, step in enumerate(STEPS):
+            if step[0] == j:
+                share(n)
+    for n in range(len(STEPS)):
+        take_share(n)
+        interfere(n)
+        if n == 1:
+            send_early()
+        if n > 1:
+            send_last(n - 2)
     for j in range(CHUNKS):
         turn_wait(j, turn_send)
-        whole = gat[j].at[pl.ds(0, ACQ - 1)]
-        pltpu.make_async_copy(whole, whole, acq_send.at[j]).wait()
+    for n in range(len(STEPS)):
+        whole = gat[n].at[pl.ds(0, ACQ - 1)]
+        pltpu.make_async_copy(whole, whole, acq_send.at[n]).wait()
     which = lax.broadcasted_iota(jnp.int32, (8, 128), 0)
     mask = lax.broadcasted_iota(jnp.int32, (8, 128), 1) // 16 == which
 
@@ -439,7 +462,7 @@
 
         @pl.when(has_own)
         def _():
-            own_out(j, first).wait()
+            own_out(j).wait()
 
         arrange(out, chunks)
 
@@ -468,11 +491,10 @@
             vmem((CHUNKS, 2, NA, 128), f32),
             vmem((CHUNKS, NA, 128), f32),
             vmem((CHUNKS, 2, AOI + 16, 128), f32),
-            vmem((ACQ, 2, PART, 128), f32),
-            vmem((ACQ, 2, PART, 128), f32),
-            vmem((ACQ, 2, PART, 128), f32),
+            *[vmem((ACQ, 2, step[1], 128), f32) for step in STEPS],
             vmem((3, 2, ACQ * PART, 128), f32),
-            vmem((CHUNKS, 2, DESTS, 1, 128), f32),
+            vmem((2, 2, DESTS, 1, 128), f32),
+            vmem((2, 2, DESTS // 2, 1, 128), f32),
             vmem((CHUNKS, 2, DESTS, 1, 128), f32),
             vmem((2, NP, NQ), f32),
             vmem((NQ, 128), f32),
@@ -495,9 +517,9 @@
             dma((CHUNKS,)),
             dma((CHUNKS,)),
             dma,
-            dma((CHUNKS,)),
-            dma((CHUNKS,)),
-            dma((CHUNKS,)),
+            dma((len(STEPS),)),
+            dma((len(STEPS),)),
+            dma((len(STEPS),)),
             dma((CHUNKS,)),
             dma((CHUNKS,)),
             dma((CHUNKS,)),

time: 83.2 us -> 81.7 us (0.982)
  Pallas kernels: 82.4 us -> 81 us
    pallas_call x1, Pallas kernels: 82.4 us -> 81 us  [shards(): pl.pallas_call(kernel, out_shape=[vmem((2 * 2 * 12 * 4, 128), f32)] * 2,...]
where the time goes in v5:
time: 81.7 us; the launch traced here: 81.6 us
  Pallas kernels  81 us (99%)
    pallas_call x1, Pallas kernels, shards(): pl.pallas_call(kernel, out_shape=[vmem((2 * 2 * 12 * 4, 128), f32)] * 2,...  81 us

profile of v5, /device:TPU:1, one launch (start us, length us, event | category | flops | bytes accessed | tf_op | source)
XLA Modules:
  0.0 81.6 jit_solution(6195811513006873248)
XLA Ops:
  0.0 81.0 %range_doppler.1 = (f32[192,128]{1,0:T(8,128)S(1)}, f32[192,128]{1,0:T(8,128)S(1)}) custom-call(s32[2,8]{1,0:T(2,128)} %pairs.1, f32[2,3,768,128]{3,2,1,0:T(8,128)} %bitcast.12, f32[2,96,128]{2,1,0:T(8,128)} %bitcast.14, f32[768,384]{1,0:T(8,128)} %bitcast.13, f32[192,576]{1,0:T(8,128)} %constant.10.clone.left_p_h, f32[256,256]{1,0:T(8,128)} %constant.11.clone.right_q_h, ...), custom_call_target="tpu_custom_call" | custom-call | tf_op jit(solution)/shard_map/range_doppler/pallas_call | solution.py:482
  81.0 0.7 add.3
